TPU v7x, 32 devices: a whole 2x2x4 slice. The times are simulated.
32 devices in a mesh: wide: 8 (over y, x, core), narrow: 4 (over z).
Axes of the slice: x: 2, y: 2, z: 4, core: 2. Of those that a mesh axis runs over, the one named last changes fastest.
Arguments:
- tokens: bfloat16 [16384, 768], P(('wide', 'narrow')), may hold values from -6 to 6
- block_size: int32 [8], P('wide'), may hold values from 4 to 16, as said below
- ln1_gain: bfloat16 [768], replicated, may hold values from 0.5 to 1.5
- ln1_shift: bfloat16 [768], replicated, may hold values from -1.5 to 1.5
- qkv_weight: bfloat16 [768, 3, 768], P(None, None, 'narrow'), may hold values from -0.21875 to 0.21875
- qkv_bias: bfloat16 [3, 768], P(None, 'narrow'), may hold values from -1.5 to 1.5
- out_weight: bfloat16 [768, 768], P('narrow'), may hold values from -1.75 to 1.75
- out_bias: bfloat16 [768], replicated, may hold values from -1.5 to 1.5
- ln2_gain: bfloat16 [768], replicated, may hold values from 0.5 to 1.5
- ln2_shift: bfloat16 [768], replicated, may hold values from -1.5 to 1.5
- up_weight: bfloat16 [768, 3072], P(None, 'narrow'), may hold values from -0.21875 to 0.21875
- up_bias: bfloat16 [3072], P('narrow'), may hold values from -1.5 to 1.5
- down_weight: bfloat16 [3072, 768], P('narrow'), may hold values from -0.109375 to 0.109375
- down_bias: bfloat16 [768], replicated, may hold values from -1.5 to 1.5
- cotangent: bfloat16 [16384, 768], P(('wide', 'narrow')), may hold values from -6 to 6
Outputs:
- activations: bfloat16 [16384, 768], P(('wide', 'narrow'))
- tokens_grad: bfloat16 [16384, 768], P(('wide', 'narrow'))
- grad_ln1_gain: float32 [768], replicated
- grad_ln1_shift: float32 [768], replicated
- grad_qkv_weight: float32 [768, 3, 768], P(None, None, 'narrow')
- grad_qkv_bias: float32 [3, 768], P(None, 'narrow')
- grad_out_weight: float32 [768, 768], P('narrow')
- grad_out_bias: float32 [768], replicated
- grad_ln2_gain: float32 [768], replicated
- grad_ln2_shift: float32 [768], replicated
- grad_up_weight: float32 [768, 3072], P(None, 'narrow')
- grad_up_bias: float32 [3072], P('narrow')
- grad_down_weight: float32 [3072, 768], P('narrow')
- grad_down_bias: float32 [768], replicated
Inputs may be any that keep to these rules, and one draw needn't show every extreme that they name: `block_size`: each sequence's block size is 4, 8 or 16, and each of the three is some sequence's.
All inputs are finite; a program needn't handle non-finite values.
Results may differ from a plain program's by a relative error of at most 0.02.
Values may be sent and summed in bfloat16 or wider, within the bound.
A program may use at most 192 MiB of HBM per device.

v0:
```python
import itertools

import jax
import jax.numpy as jnp
import numpy as np
from jax import lax
from jax.experimental import pallas as pl
from jax.experimental.pallas import tpu as pltpu
from jax.sharding import PartitionSpec as P

HEAD_DIM = 64
MESH = pl.DeviceIdType.MESH
F32 = jnp.float32
BF16 = jnp.bfloat16
NEG = -1e30
EPS = 1e-05
T = 128
C = 256
Q, O, U0, U1, D0, D1, Q0, Q1, Q2 = range(9)
GEO = ((Q, 9, 16), (O, 3, 16), (U0, 1, 96), (U1, 1, 96), (D0, 1, 96), (D1, 1, 96))
RED = (
    (D0, 1, 96), (D1, 1, 96), (U0, 1, 96), (U1, 1, 96),
    (O, 3, 16), (Q0, 3, 16), (Q1, 3, 16), (Q2, 3, 16),
)
DIRECT = (O, Q0, Q1, Q2)


def mm(a, b):
    return lax.dot_general(a, b, (((1,), (0,)), ((), ())), preferred_element_type=F32)


def mm_nt(a, b):
    return lax.dot_general(a, b, (((1,), (1,)), ((), ())), preferred_element_type=F32)


def mm_tn(a, b):
    return lax.dot_general(a, b, (((0,), (0,)), ((), ())), preferred_element_type=F32)


def norm_stats(v):
    mean = jnp.mean(v, axis=-1, keepdims=True)
    cen = v - mean
    inv = lax.rsqrt(jnp.mean(cen * cen, axis=-1, keepdims=True) + EPS)
    return cen * inv, inv


def norm_back(grad, normed, inv, gain):
    g = grad * gain
    return inv * (
        g
        - jnp.mean(g, axis=-1, keepdims=True)
        - normed * jnp.mean(g * normed, axis=-1, keepdims=True)
    )


def swap_halves(v):
    lane = lax.broadcasted_iota(jnp.int32, v.shape, 1)
    low = lax.rem(lane, 64) < 32
    return jnp.where(low, pltpu.roll(v, 96, 1), pltpu.roll(v, 32, 1))


def tables(half_len):
    freqs = np.exp(
        np.arange(HEAD_DIM // 2, dtype=np.float32)
        * np.float32(-2.0 * np.log(10000.0) / HEAD_DIM)
    ).astype(np.float32)
    angles = np.arange(half_len, dtype=np.float32)[:, None] * freqs[None, :]
    angles = angles.astype(np.float32)
    cos, sin = np.cos(angles), np.sin(angles)
    return (
        np.concatenate([cos, cos, cos, cos], 1).astype(np.float32),
        np.concatenate([-sin, sin, -sin, sin], 1).astype(np.float32),
    )


def layer_kernel(
    cos_ref, sin_ref, g1_ref, s1_ref, ob_ref, g2_ref, s2_ref, db_ref, upb_ref, qkvb_ref, bs_ref,
    tok_ref, cot_ref, in_q, in_o, in_u, in_d,
    act_out, tgrad_out, small_out, fin_q, fin_o, fin_u, fin_d,
    x, a1, qs, ks, vs, att, lse, hid, a2, gelu, gp, cot,
    w_q, w_o, w_u, w_d, g_q, g_d,
    bias_own, biases, bs_own, bs_buf, m_same, m_lt, m_le,
    e1s, e1r, e2s, e2r, e3r, e4r, ybuf, hals, halr, halz, tg, dk, dv,
    *rest,
):
    sm, smr, smz, ub, qb, ss, rs, ls = rest[-8:]
    RA, RB, RC, RD = ({g: rest[4 * k + i] for k, (g, _, _) in enumerate(RED)} for i in range(4))
    R = tok_ref.shape[0]
    D = tok_ref.shape[1]
    w = lax.axis_index("wide")
    z = lax.axis_index("narrow")
    c = lax.rem(w, 2)
    xx = lax.rem(lax.div(w, 2), 2)
    yy = lax.rem(lax.div(w, 4), 2)
    t = lax.div(z, 2)
    h = lax.rem(z, 2)
    wc = w + 1 - 2 * c
    wx = w + 2 - 4 * xx
    wy = w + 4 - 8 * yy
    z1 = z + 1 - 2 * h
    z2 = z + 2 - 4 * t
    z3 = 3 - z
    entry = 2 - c
    far = 3 - 3 * c
    home = c == t
    away = jnp.logical_not(home)
    is_entry = z == entry
    is_far = z == far

    sends, recvs, locals_ = itertools.count(), itertools.count(), itertools.count()
    pending = []

    def take(counter, n=1):
        first = next(counter)
        for _ in range(n - 1):
            next(counter)
        return first

    def when(cond, fn):
        if cond is None:
            fn()
        else:
            @pl.when(cond)
            def _():
                fn()

    def remote(src, dst, si, ri, dev):
        return pltpu.make_async_remote_copy(
            src_ref=src, dst_ref=dst, send_sem=ss.at[si], recv_sem=rs.at[ri],
            device_id=dev, device_id_type=MESH,
        )

    def send(src, dst, ri, dev, cond=None, group=pending):
        cp = remote(src, dst, take(sends), ri, dev)
        when(cond, lambda: cp.start())
        group.append((cond, lambda: cp.wait_send()))

    def sent(group):
        for cond, wait in group:
            when(cond, wait)
        group.clear()

    def recv(dst, ri, cond=None):
        cp = remote(dst, dst, 0, ri, (wc, z))
        when(cond, lambda: cp.wait_recv())

    def local(src, dst, cond=None):
        cp = pltpu.make_async_copy(src, dst, ls.at[take(locals_)])
        when(cond, lambda: cp.start())
        return lambda: when(cond, lambda: cp.wait())

    def rows(start, n):
        return pl.ds(pl.multiple_of(start, 128), n)

    def loop(lo, hi, fn):
        def step(i, _):
            fn(i)
            return 0

        lax.fori_loop(lo, hi, step, 0)

    W, IN = {Q: w_q, O: w_o}, {Q: in_q, O: in_o}
    G, FIN = {O: w_o}, {O: fin_o}
    for k in range(2):
        half = pl.ds(k, 1)
        u, d = (U0, U1)[k], (D0, D1)[k]
        W[u], W[d] = w_u.at[half], w_d.at[half]
        IN[u], IN[d] = in_u.at[half], in_d.at[half]
        G[u], G[d] = w_u.at[half], g_d.at[half]
        FIN[u], FIN[d] = fin_u.at[half], fin_d.at[half]
    for p in range(3):
        G[Q0 + p] = g_q.at[:, p]
        FIN[Q0 + p] = fin_q.at[:, p]
    HC = 6 * HEAD_DIM
    NP = HC // 128
    NC = 2 * R // C
    HB = R // C

    barrier = pltpu.get_barrier_semaphore()
    wd = wx + 4 - 8 * yy
    plane = [(wc, z), (wx, z), (wy, z), (wd, z)]
    plane += [(v + 1 - 2 * c, z) for v in (wx, wy, wd)]
    partners = plane + [(w, z1), (w, z2), (w, z3), (wc, z2), (wc, z3)]
    for dev in partners:
        pl.semaphore_signal(barrier, inc=1, device_id=dev, device_id_type=MESH)
    pl.semaphore_wait(barrier, len(partners))

    w_native = {}
    w_sent = {g: [] for g, _, _ in GEO}
    wz_r = {g: take(recvs, 2) for g, _, _ in GEO}
    wxy_r = {g: take(recvs, 6) for g, _, _ in GEO}

    def weights_out(g, group=pending):
        src = IN[g].at[:, yy, xx]
        dst = W[g].at[:, h, yy, xx]
        send(src, dst, wz_r[g] + h, (w, entry), home, group)
        send(src, dst, wz_r[g] + h, (w, z1), home, group)

    def weights_native(g):
        w_native[g] = local(IN[g], W[g].at[:, h], home)

    def foreign(s):
        return jnp.logical_not(jnp.logical_and(home, h == s))

    def weights_spread(g):
        for s in range(2):
            piece = W[g].at[:, s, yy, xx]
            recv(piece, wz_r[g] + s, foreign(s))
            for j, dev in enumerate((wx, wy)):
                send(piece, piece, wxy_r[g] + 3 * s + j, (dev, z), foreign(s), w_sent[g])
            send(piece, piece, wz_r[g] + s, (w, far), is_entry, w_sent[g])

    def weights_relay(g):
        piece = W[g].at[:, 0, yy, 1 - xx]
        recv(piece, wxy_r[g], foreign(0))
        send(piece, piece, wxy_r[g] + 2, (wy, z), foreign(0), w_sent[g])
        piece = W[g].at[:, 1, 1 - yy, xx]
        recv(piece, wxy_r[g] + 4, foreign(1))
        send(piece, piece, wxy_r[g] + 5, (wx, z), foreign(1), w_sent[g])

    def weights_wait(g):
        w_native[g]()
        recv(W[g].at[:, 0, 1 - yy, xx], wxy_r[g] + 1, foreign(0))
        recv(W[g].at[:, 0, 1 - yy, 1 - xx], wxy_r[g] + 2, foreign(0))
        recv(W[g].at[:, 1, yy, 1 - xx], wxy_r[g] + 3, foreign(1))
        recv(W[g].at[:, 1, 1 - yy, 1 - xx], wxy_r[g] + 5, foreign(1))

    bs_own[...] = jnp.full(bs_own.shape, bs_ref[0], jnp.int32)
    bs_r = take(recvs)
    send(bs_own, bs_buf, bs_r, (wc, z))

    halves = [pl.ds(k * (R // 2), R // 2) for k in range(2)]

    def block(ref, b, k):
        return ref.at[pl.ds(pl.multiple_of(R * b + k * (R // 2), 128), R // 2)]

    tok_r = take(recvs, 6)
    tok_local = local(tok_ref, x.at[pl.ds(pl.multiple_of(R * c, 128), R)], home)
    slot = (1 - c) * (4 - z)
    zt = (1 - c) + c * (z + 2)
    halo_src = jnp.logical_and(c == 1, z == 2)
    def tokens_out(k):
        src = tok_ref.at[halves[k]]
        send(src, block(x, slot, k), tok_r + 2 * slot + k, (wc, zt), away)

    def tokens_home():
        for k in range(2):
            send(tok_ref.at[halves[k]], block(x, c, k), tok_r + 2 * c + k, (wc, z), home)
        for g, _, _ in GEO:
            weights_native(g)

    def halo_out(k):
        send(tok_ref.at[halves[k]], block(x, 2, k), tok_r + 4 + k, (w, 3), halo_src)

    params = (g1_ref, s1_ref, ob_ref, g2_ref, s2_ref, db_ref, upb_ref)

    def param(k):
        return params[k][...].astype(F32).reshape(1, D)

    bias_r = take(recvs, 2)
    bias_sent = []

    def place():
        row_i = lax.broadcasted_iota(jnp.int32, (HC // 2, HC), 0)
        col_i = lax.broadcasted_iota(jnp.int32, (HC // 2, HC), 1)
        source = lax.div(col_i, 128) * HEAD_DIM + lax.rem(col_i, HEAD_DIM)
        mine = lax.div(lax.rem(col_i, 128), HEAD_DIM) == h
        return jnp.logical_and(source == row_i, mine).astype(F32)

    def biases_out():
        bias_own[...] = jnp.zeros(bias_own.shape, F32)
        bias_own[0:3, 0:HC] = mm(qkvb_ref[...], place().astype(BF16))
        bias_own[3:4, pl.ds(pl.multiple_of(h * D, 128), D)] = param(6)
        for dz in (entry, z1, far):
            send(bias_own, biases.at[h], bias_r + h, (w, dz), home, bias_sent)

        @pl.when(home)
        def _():
            biases[h] = bias_own[...]

        @pl.when(h == 0)
        def _():
            x[pl.ds(2 * R, R), :] = jnp.zeros((R, D), BF16)

    gain1, shift1 = param(0), param(1)

    def norm_block(b):
        def step(i):
            r = rows(R * b + i * C, C)
            normed, _inv = norm_stats(x[r, :].astype(F32))
            a1[r, :] = (normed * gain1 + shift1).astype(BF16)

        loop(0, R // C, step)

    def masks():
        recv(bs_buf, bs_r)
        pick = (t == c).astype(jnp.int32)
        bl = bs_own[0:1, :] * pick + bs_buf[0:1, :] * (1 - pick)
        bl = jnp.concatenate([bl, bl], axis=1)

        def block_of(v):
            return jnp.where(
                bl == 4,
                lax.shift_right_logical(v, 2),
                jnp.where(bl == 8, lax.shift_right_logical(v, 3), lax.shift_right_logical(v, 4)),
            )

        key_no = block_of(lax.broadcasted_iota(jnp.int32, (T, 2 * T), 0))
        row_no = block_of(lax.rem(lax.broadcasted_iota(jnp.int32, (T, 2 * T), 1), T))
        m_same[...] = jnp.where(key_no == row_no, 0.0, NEG)
        m_lt[...] = jnp.where(key_no < row_no, 0.0, NEG)
        m_le[...] = jnp.where(key_no <= row_no, 0.0, NEG)

    def norm_local():
        tok_local()
        for k in range(2):
            recv(block(x, 1 - c, k), tok_r + 2 * (1 - c) + k, away)
        norm_block(t)

    takes_halo = jnp.logical_and(c == 1, h == 1)
    feeds = jnp.logical_and(c == 1, z == 1)

    def halo_pass(k):
        recv(block(x, 2, k), tok_r + 4 + k, takes_halo)
        send(block(x, 2, k), block(x, 1, k), tok_r + 2 + k, (w, 0), feeds)
        send(block(x, 2, k), block(x, 2, k), tok_r + 4 + k, (wc, z), takes_halo)

    def tokens_pass(k):
        recv(block(x, c, k), tok_r + 2 * c + k, away)
        send(block(x, c, k), block(x, c, k), tok_r + 2 * c + k, (wc, z), away)

    cot_r = take(recvs, 4)
    cot_local = []

    def cotangents_out(k):
        src = cot_ref.at[halves[k]]
        send(src, block(cot, c, k), cot_r + 2 * c + k, (wc, z), home)
        send(src, block(cot, 1 - c, k), cot_r + 2 * (1 - c) + k, (wc, z2), away)
        cot_local.append(local(src, block(cot, c, k), home))

    def norm_other():
        for k in range(2):
            recv(block(x, 1 - c, k), tok_r + 2 * (1 - c) + k, home)
        norm_block(1 - t)

    def norm_halo():
        for k in range(2):
            recv(block(x, 2, k), tok_r + 4 + k, jnp.logical_and(c == 0, h == 1))
        norm_block(2)

    def biases_in():
        recv(biases.at[0], bias_r, foreign(0))
        recv(biases.at[1], bias_r + 1, foreign(1))
        sent(bias_sent)
        bias_own[...] = biases[0] + biases[1]


    def wq(j):
        return w_q[3 * j : 3 * j + 3].reshape(HC, D)

    def cos_sin(place, n):
        r = rows(place, n)
        return cos_ref[r, :], sin_ref[r, :]

    def project(i, halo):
        r = rows(i * C, C)
        a = a1[r, :]
        place = (i * C - 2 * R) if halo else (R * h + lax.rem(i * C, R))
        cs, sn = cos_sin(place, C)
        if not halo:
            qv = mm_nt(a, wq(0)) + bias_own[0:1, :HC]
            for p in range(NP):
                v = qv[:, p * 128 : p * 128 + 128]
                qs[p, r, :] = ((v * cs + swap_halves(v) * sn) * 0.125).astype(BF16)
        kv = mm_nt(a, wq(1)) + bias_own[1:2, :HC]
        for p in range(NP):
            v = kv[:, p * 128 : p * 128 + 128]
            ks[p, r, :] = (v * cs + swap_halves(v) * sn).astype(BF16)
        vv = mm_nt(a, wq(2)) + bias_own[2:3, :HC]
        for p in range(NP):
            vs[p, r, :] = vv[:, p * 128 : p * 128 + 128].astype(BF16)

    def project_block(b):
        loop(0, HB, lambda i: project(HB * b + i, False))

    def project_halo():
        loop(NC, NC + HB, lambda i: project(i, True))

    halo_bias = jnp.where(h == 1, 0.0, NEG).astype(F32)
    lane = lax.broadcasted_iota(jnp.int32, (1, 128), 1)
    lo_f = (lane < 64).astype(F32)
    lo_mask = lo_f.astype(BF16)
    hi_mask = (1.0 - lo_f).astype(BF16)

    def both_heads(v):
        return jnp.concatenate([v * lo_mask, v * hi_mask], axis=0)

    def one_of_each(v):
        return v[:T] * lo_f + v[T:] * (1.0 - lo_f)

    def key_parts(b, i):
        parts = []
        if b == 0:
            parts.append((T * i, T, m_same))
        if i > 0:
            parts.append((R, T * i, None))
        parts.append((R + T * i, T, m_lt if b == 0 else m_le))
        parts.append((2 * R, R, halo_bias))
        return parts

    def scores_of(p, part, qm):
        start, n, mask = part
        sc = mm_nt(ks[p, pl.ds(start, n), :], qm)
        if mask is None:
            return sc
        if mask is halo_bias:
            return sc + halo_bias
        return sc + mask[...]

    chunks = [(b, i) for b in range(2) for i in range(R // T)]

    def attend(p, n):
        for b, i in chunks[n : n + 1]:
            r = pl.ds(R * b + T * i, T)
            qm = both_heads(qs[p, r, :])
            parts = key_parts(b, i)
            sc = [scores_of(p, part, qm) for part in parts]
            top = None
            for v in sc:
                m = jnp.max(v, axis=0, keepdims=True)
                top = m if top is None else jnp.maximum(top, m)
            total, out = None, None
            for part, v in zip(parts, sc):
                e = jnp.exp(v - top)
                l = jnp.sum(e, axis=0, keepdims=True)
                o = mm_tn(vs[p, pl.ds(part[0], part[1]), :], e.astype(BF16))
                total = l if total is None else total + l
                out = o if out is None else out + o
            out = out / total
            att[p, r, :] = one_of_each(out.T).astype(BF16)
            lse[p, n] = top + jnp.log(total)

    e1_r = take(recvs, 4)
    e1_s = take(sends, 4)
    def swap_out(i, dst, si, ri):
        r = rows(i * C, C)
        remote(e1s.at[r], dst.at[r], si + i, ri + i, (wc, z)).start()

    def swap_in(i, dst, ri):
        r = rows(i * C, C)
        remote(dst.at[r], dst.at[r], 0, ri + i, (wc, z)).wait_recv()

    def swap_done(i, dst, si):
        r = rows(i * C, C)
        remote(e1s.at[r], dst.at[r], si + i, 0, (wc, z)).wait_send()

    def pairs(ref, r):
        return jnp.concatenate([ref[p, r, :] for p in range(NP)], axis=1)

    def out_project(i):
        r = rows(i * C, C)
        e1s[r, :] = mm(pairs(att, r), w_o[...].reshape(HC, D)).astype(BF16)
        swap_out(i, e1r, e1_s, e1_r)


    def clear():
        sm[...] = jnp.zeros(sm.shape, F32)
        ub[...] = jnp.zeros(ub.shape, F32)
        qb[...] = jnp.zeros(qb.shape, F32)

    out_bias, gain2, shift2, down_bias = param(2), param(3), param(4), param(5)
    KG = float(np.sqrt(2.0 / np.pi))

    def wu(s):
        return jnp.concatenate([w_u[0, s].reshape(D // 2, D), w_u[1, s].reshape(D // 2, D)], axis=0)

    def wd(s):
        return jnp.concatenate([w_d[0, s].reshape(D // 2, D), w_d[1, s].reshape(D // 2, D)], axis=0)

    def feed(i):
        r = rows(i * C, C)
        swap_in(i, e1r, e1_r)
        hv = x[r, :].astype(F32) + e1s[r, :].astype(F32) + e1r[r, :].astype(F32) + out_bias
        hid[r, :] = hv
        normed, _inv = norm_stats(hv)
        act = (normed * gain2 + shift2).astype(BF16)
        a2[r, :] = act
        for s in range(2):
            cols = pl.ds(s * D, D)
            u = mm(act, wu(s)) + bias_own[3:4, s * D : (s + 1) * D]
            u2 = u * u
            th = jnp.tanh(KG * u * (1.0 + 0.044715 * u2))
            half = 0.5 * (1.0 + th)
            gelu[r, cols] = (u * half).astype(BF16)
            slope = half + 0.5 * u * (1.0 - th * th) * (KG * (1.0 + 3 * 0.044715 * u2))
            gp[r, cols] = slope.astype(BF16)

    def cot_pass(k):
        cot_local[k]()
        recv(block(cot, c, k), cot_r + 2 * c + k, away)
        send(block(cot, c, k), block(cot, c, k), cot_r + 2 * c + k, (wc, z), away)

    def cot_in():
        for k in range(2):
            recv(block(cot, 1 - c, k), cot_r + 2 * (1 - c) + k)

    ra_r = {g: take(recvs, 2) for g, _, _ in RED}
    rb_r = {g: take(recvs, 2) for g, _, _ in RED}
    rc_r = {g: take(recvs, 2) for g, _, _ in RED}
    rd_r = {g: take(recvs, 2) for g, _, _ in RED}
    fin_r = {g: take(recvs, 4) for g, _, _ in RED}
    fin_local = {}
    size = {g: (n, r) for g, n, r in RED}
    turn = {g: k % 2 for k, (g, _, _) in enumerate(RED)}

    def add(dst, src):
        dst[...] = (dst[...].astype(F32) + src[...].astype(F32)).astype(BF16)

    def reduce_a(g):
        send(G[g].at[:, 0, :, 1 - xx], RA[g].at[0], ra_r[g], (wx, z))
        send(G[g].at[:, 1, 1 - yy, :], RA[g].at[1], ra_r[g] + 1, (wy, z))

    def reduce_b(g):
        n, r = size[g]
        recv(RA[g].at[0], ra_r[g])
        for k in range(n):
            add(G[g].at[k, 0, 1 - yy, xx], RA[g].at[0, k, 1 - yy])
        send(G[g].at[:, 0, 1 - yy, xx], RB[g].at[0], rb_r[g], (wy, z))
        recv(RA[g].at[1], ra_r[g] + 1)
        for k in range(n):
            add(G[g].at[k, 1, yy, 1 - xx], RA[g].at[1, k, 1 - xx])
        send(G[g].at[:, 1, yy, 1 - xx], RB[g].at[1], rb_r[g] + 1, (wx, z))
        for k in range(n):
            add(G[g].at[k, 0, yy, xx], RA[g].at[0, k, yy])
            add(G[g].at[k, 1, yy, xx], RA[g].at[1, k, xx])

    def reduce_c(g):
        n, r = size[g]
        for s in range(2):
            recv(RB[g].at[s], rb_r[g] + s)
            for k in range(n):
                add(G[g].at[k, s, yy, xx], RB[g].at[s, k])
            piece = G[g].at[:, s, yy, xx]
            if g in DIRECT:
                at = (w, 2 * c + s)
                send(piece, RC[g].at[0], rc_r[g], at, is_far)
                send(piece, RD[g].at[1], rd_r[g] + 1, at, is_entry)
            else:
                send(piece, RC[g].at[s], rc_r[g] + s, (w, entry), is_far)
            send(piece, RD[g].at[0], rd_r[g], (w, z1), jnp.logical_and(home, h == 1 - s))

    def reduce_d(g):
        n, r = size[g]
        if g in DIRECT:
            return
        for s in range(2):
            recv(RC[g].at[s], rc_r[g] + s, is_entry)

            @pl.when(is_entry)
            def _():
                for k in range(n):
                    add(G[g].at[k, s, yy, xx], RC[g].at[s, k])

            send(G[g].at[:, s, yy, xx], RD[g].at[1], rd_r[g] + 1, (w, 2 * c + s), is_entry)

    def reduce_e(g):
        n, r = size[g]
        recv(RD[g].at[0], rd_r[g], home)
        recv(RD[g].at[1], rd_r[g] + 1, home)
        if g in DIRECT:
            recv(RC[g].at[0], rc_r[g], home)

        @pl.when(home)
        def _():
            for k in range(n):
                dst = G[g].at[k, h, yy, xx]
                v = dst[...].astype(F32) + RD[g][0, k].astype(F32) + RD[g][1, k].astype(F32)
                if g in DIRECT:
                    v = v + RC[g][0, k].astype(F32)
                dst[...] = v.astype(BF16)

        piece = G[g].at[:, h, yy, xx]
        out = FIN[g].at[:, yy, xx]
        fin_local[g] = local(piece, out, home)
        for j, dev in enumerate((wx, wy)):
            send(piece, out, fin_r[g] + j, (dev, z), home)
        send(piece, out, fin_r[g] + 3, (wc, z), home)

    def reduce_f(g):
        for j, (py, px) in enumerate(((yy, 1 - xx), (1 - yy, xx))):
            piece = FIN[g].at[:, py, px]
            recv(piece, fin_r[g] + j, home)
            if j == turn[g]:
                send(piece, piece, fin_r[g] + 2, ((wy, wx)[j], z), home)
            send(piece, piece, fin_r[g] + j, (wc, z), home)

    def reduce_g(g):
        piece = FIN[g].at[:, 1 - yy, 1 - xx]
        recv(piece, fin_r[g] + 2, home)
        send(piece, piece, fin_r[g] + 2, (wc, z), home)

    def reduce_h(g):
        fin_local[g]()
        for j, (py, px) in enumerate(((yy, 1 - xx), (1 - yy, xx), (1 - yy, 1 - xx), (yy, xx))):
            recv(FIN[g].at[:, py, px], fin_r[g] + j, away)

    def grad_down(half, s):
        cols = pl.ds(pl.multiple_of(s * D + half * (D // 2), 128), D // 2)
        g = mm_tn(gelu[:, cols], cot[...])
        g_d[half, s] = g.astype(BF16).reshape(2, 2, 96, D)

    def grad_up(half, s):
        g = mm_tn(
            a2[:, half * (D // 2) : (half + 1) * (D // 2)],
            gp[:, pl.ds(pl.multiple_of(s * D, 128), D)],
        )
        w_u[half, s] = g.astype(BF16).reshape(2, 2, 96, D)

    def grads_down(half):
        loop(0, 2, lambda s: grad_down(half, s))

    def grads_up(half):
        sent(w_sent[U0 + half])
        loop(0, 2, lambda s: grad_up(half, s))

    e3_r, e3_s = take(recvs, 4), take(sends, 4)

    def back_up(i):
        r = rows(i * C, C)
        cv = cot[r, :]
        out = None
        for s in range(2):
            cols = pl.ds(s * D, D)
            gu = (mm_nt(cv, wd(s)) * gp[r, cols].astype(F32)).astype(BF16)
            gp[r, cols] = gu
            ub[0:1, cols] += jnp.sum(gu.astype(F32), axis=0, keepdims=True)
            o = mm_nt(gu, wu(s))
            out = o if out is None else out + o
        e1s[r, :] = out.astype(BF16)
        swap_out(i, e3r, e3_s, e3_r)

    def backs_up():
        loop(0, NC, lambda i: swap_done(i, e1r, e1_s))
        loop(0, NC, back_up)

    e2_r, e2_s = take(recvs, 2), take(sends, 2)

    def down_of(r):
        return mm(gelu[r, 0:D], wd(0)) + mm(gelu[r, D : 2 * D], wd(1))

    def down_other(i):
        r = rows(R * (1 - c) + i * C, C)
        d = rows(i * C, C)
        e2s[d, :] = down_of(r).astype(BF16)
        remote(e2s.at[d], e2r.at[d], e2_s + i, e2_r + i, (wc, z)).start()

    def down_own(i):
        r = rows(R * c + i * C, C)
        d = rows(i * C, C)
        part = down_of(r)
        remote(e2r.at[d], e2r.at[d], 0, e2_r + i, (wc, z)).wait_recv()
        y = hid[r, :] + part + e2r[d, :].astype(F32) + down_bias
        ybuf[d, :] = y.astype(BF16)
        sm[5:6, :] += jnp.sum(cot[r, :].astype(F32), axis=0, keepdims=True)

    z_orig = 2 * c + h
    y_r = take(recvs)
    y_local = []

    def down_mine():
        loop(0, HB, down_own)
        y_local.append(local(ybuf, act_out, home))
        send(ybuf, act_out, y_r, (wc, z_orig), away)

    def norm2_back(i):
        r = rows(i * C, C)
        swap_in(i, e3r, e3_r)
        g2 = e1s[r, :].astype(F32) + e3r[r, :].astype(F32)
        normed, inv = norm_stats(hid[r, :])
        gh = cot[r, :].astype(F32) + norm_back(g2, normed, inv, gain2)
        hid[r, :] = gh
        own = (lax.div(i, HB) == c).astype(F32)
        sm[3:4, :] += own * jnp.sum(g2 * normed, axis=0, keepdims=True)
        sm[4:5, :] += own * jnp.sum(g2, axis=0, keepdims=True)
        sm[2:3, :] += own * jnp.sum(gh, axis=0, keepdims=True)
        swap_done(i, e3r, e3_s)
        br = gh.astype(BF16)
        e1s[r, :] = br
        a2[r, 0:HC] = mm_nt(br, w_o[...].reshape(HC, D)).astype(BF16)

    def grad_out():
        everything = pl.ds(0, 2 * R)
        sent(w_sent[O])
        g_out = mm_tn(pairs(att, everything), e1s[...])
        w_o[...] = g_out.astype(BF16).reshape(3, 2, 2, 2, 16, D)

    def attend_back(p, n):
        if n == 0:
            dk[...] = jnp.zeros(dk.shape, F32)
            dv[...] = jnp.zeros(dv.shape, F32)
        for b, i in chunks[n : n + 1]:
            r = pl.ds(R * b + T * i, T)
            qm = both_heads(qs[p, r, :])
            gm = both_heads(a2[r, p * 128 : p * 128 + 128])
            parts = key_parts(b, i)
            log_total = lse[p, n]
            delta, probs, gprobs = None, [], []
            for part in parts:
                pr = jnp.exp(scores_of(p, part, qm) - log_total)
                dp = mm_nt(vs[p, pl.ds(part[0], part[1]), :], gm)
                dl = jnp.sum(pr * dp, axis=0, keepdims=True)
                delta = dl if delta is None else delta + dl
                probs.append(pr)
                gprobs.append(dp)
            dq = None
            for part, pr, dp in zip(parts, probs, gprobs):
                k = pl.ds(part[0], part[1])
                ds = (pr * (dp - delta)).astype(BF16)
                dv[k, :] += mm(pr.astype(BF16), gm)
                dk[k, :] += mm(ds, qm)
                d = mm_tn(ks[p, k, :], ds)
                dq = d if dq is None else dq + d
            dq = one_of_each(dq.T) * 0.125
            cs, sn = cos_sin(R * h + T * i, T)
            dq = (dq * cs - swap_halves(dq) * sn).astype(BF16)
            qs[p, r, :] = dq

    def attend_end(p):
        for b in range(3):
            cs, sn = cos_sin(R * h if b < 2 else 0, R)
            r = pl.ds(R * b, R)
            v = dk[r, :]
            ks[p, r, :] = (v * cs - swap_halves(v) * sn).astype(BF16)
            vs[p, r, :] = dv[r, :].astype(BF16)

    def grad_qkv(p):
        r, o = pl.ds(0, 2 * R), pl.ds(2 * R, R)
        lhs = jnp.concatenate([qs[p, r, :], ks[p, r, :], vs[p, r, :]], axis=1)
        over = jnp.concatenate([ks[p, o, :], vs[p, o, :]], axis=1)
        g = mm_tn(lhs, a1[r, :])
        g_over = mm_tn(over, a1[o, :])
        g_q[0, p] = g[:128].astype(BF16).reshape(2, 2, 2, 16, D)
        for j in range(2):
            part = g[128 * (j + 1) : 128 * (j + 2)] + g_over[128 * j : 128 * (j + 1)]
            g_q[j + 1, p] = part.astype(BF16).reshape(2, 2, 2, 16, D)
        cols = pl.ds(128 * p, 128)
        qb[0:1, cols] = jnp.sum(qs[p, r, :].astype(F32), axis=0, keepdims=True)
        qb[1:2, cols] = jnp.sum(ks[p].astype(F32), axis=0, keepdims=True)
        qb[2:3, cols] = jnp.sum(vs[p].astype(F32), axis=0, keepdims=True)

    def back_qkv(r, halo):
        g = mm(pairs(ks, r), wq(1)) + mm(pairs(vs, r), wq(2))
        return g if halo else g + mm(pairs(qs, r), wq(0))

    hal_r, hal_s = take(recvs, 2), take(sends, 2)
    halz_r = take(recvs, 2)
    e4_r, e4_s = take(recvs, 2), take(sends, 2)

    def halo_back(i):
        d = rows(i * C, C)
        hals[d, :] = back_qkv(rows(2 * R + i * C, C), True).astype(BF16)

        @pl.when(c == 0)
        def _():
            remote(hals.at[d], halr.at[d], hal_s + i, hal_r + i, (wc, z)).start()

    def halos_back():
        loop(0, HB, halo_back)

    def other_back(i):
        d = rows(i * C, C)
        e2s[d, :] = back_qkv(rows(R * (1 - c) + i * C, C), False).astype(BF16)
        remote(e2s.at[d], e4r.at[d], e4_s + i, e4_r + i, (wc, z)).start()

    def others_back():
        loop(0, HB, lambda i: remote(
            e2s.at[rows(i * C, C)], e2r.at[rows(i * C, C)], e2_s + i, 0, (wc, z)).wait_send())
        loop(0, HB, other_back)

    def halo_sum(k):
        d = pl.ds(k * C, C)
        recv(halr.at[d], hal_r + k, c == 1)

        @pl.when(c == 1)
        def _():
            add(hals.at[d], halr.at[d])

        send(hals.at[d], halz.at[d], halz_r + k, (w, z1), jnp.logical_and(c == 1, h == 1))

    def own_back(i):
        tg[rows(i * C, C), :] = back_qkv(rows(R * c + i * C, C), False)

    def owns_back():
        loop(0, HB, own_back)

        @pl.when(jnp.logical_not(gets))
        def _():
            halz[...] = jnp.zeros(halz.shape, BF16)

    gets = jnp.logical_and(c == 1, h == 0)
    t_r = take(recvs, 2)

    def norm1_back(i):
        d = pl.ds(i * C, C)
        r = rows(R * c + i * C, C)
        recv(halz.at[d], halz_r + i, gets)
        remote(e4r.at[d], e4r.at[d], 0, e4_r + i, (wc, z)).wait_recv()
        g1 = tg[d, :] + e4r[d, :].astype(F32) + halz[d, :].astype(F32)
        normed, inv = norm_stats(x[r, :].astype(F32))
        out = hid[r, :] + norm_back(g1, normed, inv, gain1)
        sm[0:1, :] += jnp.sum(g1 * normed, axis=0, keepdims=True)
        sm[1:2, :] += jnp.sum(g1, axis=0, keepdims=True)
        e1r[d, :] = out.astype(BF16)
        send(e1r.at[d], tgrad_out.at[d], t_r + i, (wc, z_orig), away)
        t_local.append(local(e1r.at[d], tgrad_out.at[d], home))

    t_local = []

    me = lax.rem(w, 8)
    base = w - me
    sm_r, sm2_r = take(recvs, 8), take(recvs, 4)

    def small_out_plane():
        cf = c.astype(F32)
        for j in range(3):
            sm[6 + j : 7 + j, 0:HC] = qb[j : j + 1, :] * (1.0 - cf)
            sm[6 + j : 7 + j, HC : 2 * HC] = qb[j : j + 1, :] * cf
        for s in range(2):
            sm[9 + s : 10 + s, :] = ub[0:1, s * D : (s + 1) * D] * (1.0 - cf)
            sm[11 + s : 12 + s, :] = ub[0:1, s * D : (s + 1) * D] * cf
        smr[me] = sm[...]
        for dev in plane:
            send(smr.at[me], smr.at[me], sm_r + me, dev)

    def small_out_z():
        for dev, _ in plane:
            other = dev - base
            recv(smr.at[other], sm_r + other)
        total = smr[0]
        for k in range(1, 8):
            total = total + smr[k]
        smz[z] = total
        for dev in (z1, z2, z3):
            send(smz.at[z], smz.at[z], sm2_r + z, (w, dev))

    def small_end():
        for dev in (z1, z2, z3):
            recv(smz.at[dev], sm2_r + dev)
        total = smz[0] + smz[1] + smz[2] + smz[3]
        sm[...] = total
        small_out[...] = total
        small_out[9:10, :] = sm[pl.ds(9 + z, 1), :]
        mine = sm[6:9, pl.ds(pl.multiple_of(HC * t, 128), HC)]
        small_out[6:9, 0 : HC // 2] = lax.dot_general(
            mine, place(), (((1,), (1,)), ((), ())), precision=lax.Precision.HIGHEST,
            preferred_element_type=F32,
        )

    weights_out(Q)
    biases_out()
    halo_out(0)
    tokens_out(0)
    halo_out(1)
    weights_spread(Q)
    halo_pass(0)
    tokens_out(1)
    tokens_pass(0)
    weights_out(O)
    tokens_home()
    weights_relay(Q)
    norm_local()
    weights_spread(O)
    masks()
    halo_pass(1)
    weights_out(U0)
    tokens_pass(1)
    weights_relay(O)
    weights_spread(U0)
    norm_halo()
    biases_in()
    weights_wait(Q)
    weights_out(U1)
    project_block(t)
    norm_other()
    weights_out(D0)
    project_block(1 - t)
    weights_spread(U1)
    project_halo()
    attend(0, 0)
    attend(0, 1)
    clear()
    cotangents_out(0)
    weights_wait(O)
    attend(0, 2)
    attend(0, 3)
    attend(0, 4)
    attend(0, 5)
    weights_relay(U0)
    attend(0, 6)
    weights_out(D1)
    attend(0, 7)
    attend(1, 0)
    attend(1, 1)
    attend(1, 2)
    attend(1, 3)
    weights_relay(U1)
    weights_spread(D0)
    attend(1, 4)
    attend(1, 5)
    attend(1, 6)
    attend(1, 7)
    attend(2, 0)
    attend(2, 1)
    attend(2, 2)
    cotangents_out(1)
    attend(2, 3)
    weights_wait(U0)
    attend(2, 4)
    attend(2, 5)
    attend(2, 6)
    weights_spread(D1)
    attend(2, 7)
    loop(0, NC, out_project)
    weights_relay(D0)
    weights_wait(U1)
    loop(0, NC, feed)
    weights_relay(D1)
    cot_pass(0)
    cot_pass(1)
    weights_wait(D0)
    cot_in()
    grads_down(0)
    weights_wait(D1)
    reduce_a(D0)
    loop(0, HB, down_other)
    grads_down(1)
    reduce_a(D1)
    backs_up()
    reduce_b(D0)
    grads_up(0)
    reduce_a(U0)
    down_mine()
    grads_up(1)
    loop(0, NC, norm2_back)
    attend_back(0, 0)
    reduce_a(U1)
    attend_back(0, 1)
    reduce_b(D1)
    attend_back(0, 2)
    attend_back(0, 3)
    attend_back(0, 4)
    attend_back(0, 5)
    reduce_c(D0)
    reduce_b(U0)
    attend_back(0, 6)
    attend_back(0, 7)
    attend_end(0)
    grad_out()
    attend_back(1, 0)
    reduce_a(O)
    attend_back(1, 1)
    reduce_c(D1)
    grad_qkv(0)
    attend_back(1, 2)
    attend_back(1, 3)
    attend_back(1, 4)
    reduce_b(U1)
    attend_back(1, 5)
    attend_back(1, 6)
    attend_back(1, 7)
    attend_end(1)
    attend_back(2, 0)
    reduce_b(O)
    reduce_d(D0)
    attend_back(2, 1)
    reduce_a(Q0)
    reduce_c(U1)
    attend_back(2, 2)
    grad_qkv(1)
    reduce_a(Q1)
    reduce_c(O)
    reduce_d(D1)
    attend_back(2, 3)
    reduce_e(D0)
    reduce_c(U0)
    attend_back(2, 4)
    attend_back(2, 5)
    attend_back(2, 6)
    attend_back(2, 7)
    attend_end(2)
    reduce_b(Q1)
    reduce_d(U1)
    reduce_b(Q0)
    halos_back()
    halo_sum(0)
    grad_qkv(2)
    reduce_e(U1)
    reduce_e(O)
    reduce_c(Q0)
    reduce_e(D1)
    halo_sum(1)
    reduce_a(Q2)
    reduce_c(Q1)
    reduce_f(O)
    others_back()
    reduce_d(U0)
    reduce_f(D0)
    reduce_b(Q2)
    reduce_e(Q0)
    reduce_g(D0)
    reduce_e(U0)
    reduce_e(Q1)
    owns_back()
    reduce_c(Q2)
    reduce_f(Q0)
    norm1_back(0)
    reduce_e(Q2)
    norm1_back(1)
    small_out_plane()
    reduce_f(Q1)
    reduce_f(Q2)
    reduce_g(O)
    reduce_g(Q0)
    reduce_g(Q2)
    reduce_f(D1)
    small_out_z()
    reduce_g(Q1)
    reduce_f(U0)
    reduce_f(U1)
    reduce_g(U0)
    reduce_g(D1)
    reduce_g(U1)
    small_end()
    for g, _, _ in RED:
        reduce_h(g)
    recv(act_out, y_r, away)
    y_local[0]()
    for k in range(HB):
        d = pl.ds(k * C, C)
        recv(tgrad_out.at[d], t_r + k, away)
        t_local[k]()
    loop(0, HB, lambda i: remote(
        e2s.at[rows(i * C, C)], e4r.at[rows(i * C, C)], e4_s + i, 0, (wc, z)).wait_send())

    @pl.when(c == 0)
    def _():
        for k in range(HB):
            d = pl.ds(k * C, C)
            remote(hals.at[d], halr.at[d], hal_s + k, 0, (wc, z)).wait_send()

    sent(w_sent[Q])
    sent(w_sent[D0])
    sent(w_sent[D1])
    sent(pending)
    counts = (next(sends), next(recvs), next(locals_))
    assert counts[0] <= ss.shape[0] and counts[1] <= rs.shape[0] and counts[2] <= ls.shape[0], counts


def shards(
    tokens, block_size, ln1_gain, ln1_shift, qkv_weight, qkv_bias, out_weight, out_bias,
    ln2_gain, ln2_shift, up_weight, up_bias, down_weight, down_bias, cotangent, groups,
):
    R, D = tokens.shape
    local_width = qkv_weight.shape[2]
    HC = 2 * local_width
    FC = 2 * up_weight.shape[1]
    cos, sin = tables(2 * R)
    wq = jnp.transpose(qkv_weight, (1, 2, 0)).reshape(9, 2, 2, 16, D)
    wo = out_weight.reshape(3, 2, 2, 16, D)
    wu = up_weight.reshape(2, 2, 2, 96, D)
    wdn = down_weight.reshape(2, 2, 2, 96, D)
    anyspec = pl.BlockSpec(memory_space=pl.ANY)
    vspec = pl.BlockSpec(memory_space=pltpu.VMEM)
    sds = jax.ShapeDtypeStruct
    fins = [sds((3, 3, 2, 2, 16, D), BF16), sds((3, 2, 2, 16, D), BF16)]
    fins += [sds((2, 2, 2, 96, D), BF16)] * 2
    V = pltpu.VMEM
    weights = [V((n, 2, 2, 2, r, D), BF16) for n, r in ((9, 16), (3, 16), (2, 96), (2, 96))]
    recvs = []
    for _, n, r in RED:
        recvs += [
            V((2, n, 2, r, D), BF16),
            V((2, n, r, D), BF16),
            V((2, n, r, D), BF16),
            V((2, n, r, D), BF16),
        ]
    NP = HC // 128
    outs = pl.pallas_call(
        layer_kernel,
        out_shape=[sds((R, D), BF16), sds((R, D), BF16), sds((16, D), F32)] + fins,
        in_specs=[vspec] * 10 + [pl.BlockSpec(memory_space=pltpu.SMEM)] + [anyspec] * 6,
        out_specs=[anyspec, anyspec, vspec] + [anyspec] * 4,
        scratch_shapes=[
            V((3 * R, D), BF16),
            V((3 * R, D), BF16),
            V((NP, 2 * R, 128), BF16),
            V((NP, 3 * R, 128), BF16),
            V((NP, 3 * R, 128), BF16),
            V((NP, 2 * R, 128), BF16),
            V((NP, 2 * R // T, 1, 2 * T), F32),
            V((2 * R, D), F32),
            V((2 * R, D), BF16),
            V((2 * R, FC), BF16),
            V((2 * R, FC), BF16),
            V((2 * R, D), BF16),
            *weights,
            V((3, 3, 2, 2, 2, 16, D), BF16),
            V((2, 2, 2, 2, 96, D), BF16),
            V((8, FC), F32),
            V((2, 8, FC), F32),
            V((8, 128), jnp.int32),
            V((8, 128), jnp.int32),
            V((T, 2 * T), F32),
            V((T, 2 * T), F32),
            V((T, 2 * T), F32),
            V((2 * R, D), BF16),
            V((2 * R, D), BF16),
            V((R, D), BF16),
            V((R, D), BF16),
            V((2 * R, D), BF16),
            V((R, D), BF16),
            V((R, D), BF16),
            V((R, D), BF16),
            V((R, D), BF16),
            V((R, D), BF16),
            V((R, D), F32),
            V((3 * R, 128), F32),
            V((3 * R, 128), F32),
            *recvs,
            V((16, D), F32),
            V((8, 16, D), F32),
            V((4, 16, D), F32),
            V((8, FC), F32),
            V((8, HC), F32),
            pltpu.SemaphoreType.DMA((260,)),
            pltpu.SemaphoreType.DMA((220,)),
            pltpu.SemaphoreType.DMA((24,)),
        ],
        compiler_params=pltpu.CompilerParams(
            collective_id=0, has_side_effects=True, vmem_limit_bytes=62 * 1024 * 1024
        ),
        name="layer",
    )(
        jnp.asarray(cos), jnp.asarray(sin), ln1_gain, ln1_shift, out_bias, ln2_gain, ln2_shift,
        down_bias, up_bias, qkv_bias, block_size, tokens, cotangent, wq, wo, wu, wdn,
    )
    act, tgrad, small, fq, fo, fu, fd = outs
    grads = [
        jnp.transpose(fq.reshape(3, local_width, D), (2, 0, 1)).astype(F32),
        fo.reshape(local_width, D).astype(F32),
        fu.reshape(D, D).astype(F32),
        fd.reshape(D, D).astype(F32),
    ]
    if groups > 1:
        ids = [[g * 8 + k for g in range(groups)] for k in range(8)]
        grads, small = lax.psum((grads, small), "wide", axis_index_groups=ids)
    gq, go, gu, gd = grads
    qb, ubias = small[6:9, :local_width], small[9]
    return (
        act, tgrad, small[0], small[1], gq, qb, go, small[2], small[3], small[4], gu, ubias, gd, small[5],
    )


def solution(mesh):
    both = P(("wide", "narrow"), None)
    in_specs = (
        both, P("wide"), P(), P(), P(None, None, "narrow"), P(None, "narrow"), P("narrow", None), P(),
        P(), P(), P(None, "narrow"), P("narrow"), P("narrow", None), P(), both,
    )
    out_specs = (
        both, both, P(), P(), P(None, None, "narrow"), P(None, "narrow"), P("narrow", None), P(),
        P(), P(), P(None, "narrow"), P("narrow"), P("narrow", None), P(),
    )
    groups = mesh.shape["wide"] // 8

    def body(*args):
        return shards(*args, groups)

    return jax.shard_map(body, mesh=mesh, in_specs=in_specs, out_specs=out_specs, check_vma=False)
```

profile of v0, /device:TPU:0, one launch (start us, length us, event | category | flops | bytes accessed | tf_op | source)
XLA Modules:
  0.0 192.7 jit_solution(17169589434326546627)
XLA Ops:
  1.3 181.5 %layer.1 = (bf16[512,768]{1,0:T(8,128)(2,1)}, bf16[512,768]{1,0:T(8,128)(2,1)}, f32[16,768]{1,0:T(8,128)}, bf16[3,3,2,2,16,768]{5,4,3,2,1,0:T(8,128)(2,1)}, bf16...) custom-call(f32[1024,128]{1,0:T(8,128)} %constant.4.clone.cos_ref, ...), custom_call_target="tpu_custom_call" | custom-call | tf_op jit(solution)/shard_map/layer/pallas_call | solution.py:1088
  182.8 0.0 copy-start.4
  182.8 0.0 copy-start
  182.8 4.3 %bitcast_convert_fusion = (f32[768,768]{1,0:T(8,128)}, f32[768,768]{1,0:T(8,128)}) fusion(bf16[2,2,2,96,768]{4,3,2,1,0:T(8,128)(2,1)} %get-tuple-element.27, bf16[2,2,2,96,768]{4,3,2,1,0:T(8,128)(2,1)} %get-tuple-element.26), kind=kLoop, calls=%fused_computation.1 | loop fusion | flops 1179648 | bytes 7077888 | tf_op jit(solution)/shard_map/convert_element_type | solution.py:1152
  187.1 0.0 copy-start.3
  187.1 0.0 copy-done.4
  187.1 0.7 slice_reduce_fusion
  187.7 0.6 slice.26
  188.3 0.0 copy-done
  188.3 0.0 copy-start.2
  188.3 1.4 convert_bitcast_fusion
  189.7 0.0 copy-start.1
  189.7 0.0 copy-done.3
  189.8 0.9 bitcast_convert_fusion.2
  190.6 0.0 copy-done.2
  190.6 0.9 copy.34
  191.5 0.0 copy-done.1
  191.5 0.9 copy.35
Async XLA Ops:
  182.8 4.3 %copy-start.4 = (f32[16,768]{1,0:T(8,128)S(1)}, f32[16,768]{1,0:T(8,128)}, u32[]{:S(2)}) copy-start(f32[16,768]{1,0:T(8,128)} %get-tuple-element.23) | copy-start | bytes 147460
  182.8 5.5 %copy-start = (bf16[3,3,2,2,16,768]{5,4,3,2,1,0:T(8,128)(2,1)S(1)}, bf16[3,3,2,2,16,768]{5,4,3,2,1,0:T(8,128)(2,1)}, u32[]{:S(2)}) copy-start(bf16[3,3,2,2,16,768]{5,4,3,2,1,0:T(8,128)(2,1)} %get-tuple-element.24) | copy-start | bytes 2654212
  187.1 2.7 %copy-start.3 = (bf16[3,2,2,16,768]{4,3,2,1,0:T(8,128)(2,1)S(1)}, bf16[3,2,2,16,768]{4,3,2,1,0:T(8,128)(2,1)}, u32[]{:S(2)}) copy-start(bf16[3,2,2,16,768]{4,3,2,1,0:T(8,128)(2,1)} %get-tuple-element.25) | copy-start | bytes 884740
  188.3 2.3 %copy-start.2 = (bf16[512,768]{1,0:T(8,128)(2,1)S(1)}, bf16[512,768]{1,0:T(8,128)(2,1)}, u32[]{:S(2)}) copy-start(bf16[512,768]{1,0:T(8,128)(2,1)} %get-tuple-element.51) | copy-start | bytes 2359300
  189.7 1.8 copy-start.1
where the time goes:
time: 196 us; the launch traced here: 193 us
  Pallas kernels  181 us (92%)
  other arithmetic  6.54 us (3%)
  local copies, waits for them, and re-layouts  3.03 us (2%)
    pallas_call x1, Pallas kernels, shards(): pl.pallas_call(layer_kernel, out_shape=[sds((R, D), BF16), sds((R, D), BF...  181 us
    convert_element_type x1, other arithmetic, shards(): fd.reshape(D, D).astype(F32)  4.25 us

commit v1 on v0

--- a/solution.py
+++ b/solution.py
@@ -80,7 +80,7 @@
     x, a1, qs, ks, vs, att, lse, hid, a2, gelu, gp, cot,
     w_q, w_o, w_u, w_d, g_q, g_d,
     bias_own, biases, bs_own, bs_buf, m_same, m_lt, m_le,
-    e1s, e1r, e2s, e2r, e3r, e4r, ybuf, hals, halr, halz, tg, dk, dv,
+    turned, e1s, e1r, e2s, e2r, e3r, e4r, ybuf, hals, halr, halz, tg, dk, dv,
     *rest,
 ):
     sm, smr, smz, ub, qb, ss, rs, ls = rest[-8:]
@@ -130,14 +130,25 @@
             device_id=dev, device_id_type=MESH,
         )
 
+    most = x.shape[0]
+
     def send(src, dst, ri, dev, cond=None, group=pending):
-        cp = remote(src, dst, take(sends), ri, dev)
+        n = src.size * jnp.dtype(src.dtype).itemsize // (2 * D)
+        for entry_ in group:
+            if entry_[0] is cond and entry_[2] + n <= most:
+                entry_[2] += n
+                break
+        else:
+            entry_ = [cond, take(sends), n]
+            group.append(entry_)
+        cp = remote(src, dst, entry_[1], ri, dev)
         when(cond, lambda: cp.start())
-        group.append((cond, lambda: cp.wait_send()))
 
     def sent(group):
-        for cond, wait in group:
-            when(cond, wait)
+        for cond, si, n in group:
+            piece = x.at[pl.ds(0, n)]
+            cp = remote(piece, piece, si, 0, (wc, z))
+            when(cond, lambda: cp.wait_send())
         group.clear()
 
     def recv(dst, ri, cond=None):
@@ -199,35 +210,43 @@
     def weights_native(g):
         w_native[g] = local(IN[g], W[g].at[:, h], home)
 
+    foreign_ = [jnp.logical_not(jnp.logical_and(home, h == s)) for s in range(2)]
+
     def foreign(s):
-        return jnp.logical_not(jnp.logical_and(home, h == s))
+        return foreign_[s]
 
     def weights_spread(g):
         for s in range(2):
             piece = W[g].at[:, s, yy, xx]
             recv(piece, wz_r[g] + s, foreign(s))
+            relayed = 0 if s == 0 else 1
             for j, dev in enumerate((wx, wy)):
-                send(piece, piece, wxy_r[g] + 3 * s + j, (dev, z), foreign(s), w_sent[g])
+                r = wxy_r[g] + 3 * s + (0 if j == relayed else 2)
+                send(piece, piece, r, (dev, z), foreign(s), w_sent[g])
             send(piece, piece, wz_r[g] + s, (w, far), is_entry, w_sent[g])
 
     def weights_relay(g):
-        piece = W[g].at[:, 0, yy, 1 - xx]
-        recv(piece, wxy_r[g], foreign(0))
-        send(piece, piece, wxy_r[g] + 2, (wy, z), foreign(0), w_sent[g])
-        piece = W[g].at[:, 1, 1 - yy, xx]
-        recv(piece, wxy_r[g] + 4, foreign(1))
-        send(piece, piece, wxy_r[g] + 5, (wx, z), foreign(1), w_sent[g])
+        along_x = 0
+        piece = W[g].at[:, along_x, yy, 1 - xx]
+        r = wxy_r[g] + 3 * along_x
+        recv(piece, r, foreign(along_x))
+        send(piece, piece, r + 2, (wy, z), foreign(along_x), w_sent[g])
+        along_y = 1 - along_x
+        piece = W[g].at[:, along_y, 1 - yy, xx]
+        r = wxy_r[g] + 3 * along_y
+        recv(piece, r, foreign(along_y))
+        send(piece, piece, r + 2, (wx, z), foreign(along_y), w_sent[g])
 
     def weights_wait(g):
         w_native[g]()
-        recv(W[g].at[:, 0, 1 - yy, xx], wxy_r[g] + 1, foreign(0))
-        recv(W[g].at[:, 0, 1 - yy, 1 - xx], wxy_r[g] + 2, foreign(0))
-        recv(W[g].at[:, 1, yy, 1 - xx], wxy_r[g] + 3, foreign(1))
-        recv(W[g].at[:, 1, 1 - yy, 1 - xx], wxy_r[g] + 5, foreign(1))
+        along_x = 0
+        along_y = 1 - along_x
+        recv(W[g].at[:, along_x, 1 - yy], wxy_r[g] + 3 * along_x + 2, foreign(along_x))
+        recv(W[g].at[:, along_y, :, 1 - xx], wxy_r[g] + 3 * along_y + 2, foreign(along_y))
 
     bs_own[...] = jnp.full(bs_own.shape, bs_ref[0], jnp.int32)
-    bs_r = take(recvs)
-    send(bs_own, bs_buf, bs_r, (wc, z))
+    bs_copy = remote(bs_own, bs_buf, take(sends), take(recvs), (wc, z))
+    bs_copy.start()
 
     halves = [pl.ds(k * (R // 2), R // 2) for k in range(2)]
 
@@ -293,7 +312,7 @@
         loop(0, R // C, step)
 
     def masks():
-        recv(bs_buf, bs_r)
+        bs_copy.wait()
         pick = (t == c).astype(jnp.int32)
         bl = bs_own[0:1, :] * pick + bs_buf[0:1, :] * (1 - pick)
         bl = jnp.concatenate([bl, bl], axis=1)
@@ -411,29 +430,30 @@
     def scores_of(p, part, qm):
         start, n, mask = part
         sc = mm_nt(ks[p, pl.ds(start, n), :], qm)
-        if mask is None:
-            return sc
-        if mask is halo_bias:
-            return sc + halo_bias
-        return sc + mask[...]
+        return sc if mask is None or mask is halo_bias else sc + mask[...]
+
+    def bias_of(part):
+        return halo_bias if part[2] is halo_bias else 0.0
 
     chunks = [(b, i) for b in range(2) for i in range(R // T)]
 
     def attend(p, n):
+        if n == 0:
+            turned[...] = vs[p].T
         for b, i in chunks[n : n + 1]:
             r = pl.ds(R * b + T * i, T)
             qm = both_heads(qs[p, r, :])
             parts = key_parts(b, i)
             sc = [scores_of(p, part, qm) for part in parts]
             top = None
-            for v in sc:
-                m = jnp.max(v, axis=0, keepdims=True)
+            for part, v in zip(parts, sc):
+                m = jnp.max(v, axis=0, keepdims=True) + bias_of(part)
                 top = m if top is None else jnp.maximum(top, m)
             total, out = None, None
             for part, v in zip(parts, sc):
-                e = jnp.exp(v - top)
+                e = jnp.exp(v - (top - bias_of(part)))
                 l = jnp.sum(e, axis=0, keepdims=True)
-                o = mm_tn(vs[p, pl.ds(part[0], part[1]), :], e.astype(BF16))
+                o = mm(turned[:, pl.ds(part[0], part[1])], e.astype(BF16))
                 total = l if total is None else total + l
                 out = o if out is None else out + o
             out = out / total
@@ -508,7 +528,8 @@
     rb_r = {g: take(recvs, 2) for g, _, _ in RED}
     rc_r = {g: take(recvs, 2) for g, _, _ in RED}
     rd_r = {g: take(recvs, 2) for g, _, _ in RED}
-    fin_r = {g: take(recvs, 4) for g, _, _ in RED}
+    fin_r = {g: take(recvs, 3) for g, _, _ in RED}
+    pass_r = take(recvs, 2)
     fin_local = {}
     size = {g: (n, r) for g, n, r in RED}
     turn = {g: k % 2 for k, (g, _, _) in enumerate(RED)}
@@ -584,7 +605,7 @@
         fin_local[g] = local(piece, out, home)
         for j, dev in enumerate((wx, wy)):
             send(piece, out, fin_r[g] + j, (dev, z), home)
-        send(piece, out, fin_r[g] + 3, (wc, z), home)
+        send(piece, out, pass_r + int(g in (O, Q0, Q1, Q2)), (wc, z), home)
 
     def reduce_f(g):
         for j, (py, px) in enumerate(((yy, 1 - xx), (1 - yy, xx))):
@@ -592,17 +613,18 @@
             recv(piece, fin_r[g] + j, home)
             if j == turn[g]:
                 send(piece, piece, fin_r[g] + 2, ((wy, wx)[j], z), home)
-            send(piece, piece, fin_r[g] + j, (wc, z), home)
+            send(piece, piece, pass_r + int(g in (O, Q0, Q1, Q2)), (wc, z), home)
 
     def reduce_g(g):
         piece = FIN[g].at[:, 1 - yy, 1 - xx]
         recv(piece, fin_r[g] + 2, home)
-        send(piece, piece, fin_r[g] + 2, (wc, z), home)
-
-    def reduce_h(g):
-        fin_local[g]()
-        for j, (py, px) in enumerate(((yy, 1 - xx), (1 - yy, xx), (1 - yy, 1 - xx), (yy, xx))):
-            recv(FIN[g].at[:, py, px], fin_r[g] + j, away)
+        send(piece, piece, pass_r + int(g in (O, Q0, Q1, Q2)), (wc, z), home)
+
+    def results_in():
+        for g, _, _ in RED:
+            fin_local[g]()
+        for k, n in enumerate((2 * D, D)):
+            recv(x.at[pl.ds(0, n)], pass_r + k, away)
 
     def grad_down(half, s):
         cols = pl.ds(pl.multiple_of(s * D + half * (D // 2), 128), D // 2)
@@ -698,27 +720,30 @@
         if n == 0:
             dk[...] = jnp.zeros(dk.shape, F32)
             dv[...] = jnp.zeros(dv.shape, F32)
+            turned[...] = ks[p].T
         for b, i in chunks[n : n + 1]:
             r = pl.ds(R * b + T * i, T)
             qm = both_heads(qs[p, r, :])
-            gm = both_heads(a2[r, p * 128 : p * 128 + 128])
+            ga = a2[r, p * 128 : p * 128 + 128]
+            gm = both_heads(ga)
             parts = key_parts(b, i)
             log_total = lse[p, n]
-            delta, probs, gprobs = None, [], []
+            inner = (ga.astype(F32) * att[p, r, :].astype(F32)).T
+            delta = jnp.concatenate(
+                [
+                    jnp.sum(inner[:HEAD_DIM], axis=0, keepdims=True),
+                    jnp.sum(inner[HEAD_DIM:], axis=0, keepdims=True),
+                ],
+                axis=1,
+            )
+            dq = None
             for part in parts:
-                pr = jnp.exp(scores_of(p, part, qm) - log_total)
-                dp = mm_nt(vs[p, pl.ds(part[0], part[1]), :], gm)
-                dl = jnp.sum(pr * dp, axis=0, keepdims=True)
-                delta = dl if delta is None else delta + dl
-                probs.append(pr)
-                gprobs.append(dp)
-            dq = None
-            for part, pr, dp in zip(parts, probs, gprobs):
                 k = pl.ds(part[0], part[1])
-                ds = (pr * (dp - delta)).astype(BF16)
+                pr = jnp.exp(scores_of(p, part, qm) - (log_total - bias_of(part)))
+                ds = (pr * (mm_nt(vs[p, k, :], gm) - delta)).astype(BF16)
                 dv[k, :] += mm(pr.astype(BF16), gm)
                 dk[k, :] += mm(ds, qm)
-                d = mm_tn(ks[p, k, :], ds)
+                d = mm(turned[:, k], ds)
                 dq = d if dq is None else dq + d
             dq = one_of_each(dq.T) * 0.125
             cs, sn = cos_sin(R * h + T * i, T)
@@ -1031,8 +1056,7 @@
     reduce_g(D1)
     reduce_g(U1)
     small_end()
-    for g, _, _ in RED:
-        reduce_h(g)
+    results_in()
     recv(act_out, y_r, away)
     y_local[0]()
     for k in range(HB):
@@ -1054,6 +1078,64 @@
     sent(pending)
     counts = (next(sends), next(recvs), next(locals_))
     assert counts[0] <= ss.shape[0] and counts[1] <= rs.shape[0] and counts[2] <= ls.shape[0], counts
+
+
+def finish_kernel(
+    small_ref, q_ref, o_ref, u_ref, d_ref, act_ref, tg_ref,
+    g1, s1, ob, g2, s2, db, upb, qkvb, gq, go, gu, gd, act, tg,
+    low, high, kept, ls, ss, cs,
+):
+    n = low.shape[1]
+    parts = [
+        (src.at[pl.ds(k, n)], dst.at[pl.ds(k, n)])
+        for src, dst in ((u_ref, gu), (d_ref, gd), (o_ref, go), (q_ref, gq))
+        for k in range(0, src.shape[0], n)
+    ]
+    loads = [pltpu.make_async_copy(a, low.at[k], ls.at[k]) for k, (a, _) in enumerate(parts)]
+    stores = [pltpu.make_async_copy(high.at[k], b, ss.at[k]) for k, (_, b) in enumerate(parts)]
+    inward = [pltpu.make_async_copy(a, kept.at[k], cs.at[k]) for k, a in enumerate((act_ref, tg_ref))]
+    outward = [pltpu.make_async_copy(kept.at[k], b, cs.at[2 + k]) for k, b in enumerate((act, tg))]
+    for load in loads + inward:
+        load.start()
+    for k, out in enumerate((g1, s1, ob, g2, s2, db)):
+        out[...] = small_ref[k, :]
+    upb[...] = small_ref[9, :]
+    qkvb[...] = small_ref[6:9, : qkvb.shape[1]]
+    for k, load in enumerate(loads):
+        load.wait()
+        high[k] = low[k].astype(F32)
+        stores[k].start()
+    for load, store in zip(inward, outward):
+        load.wait()
+        store.start()
+    for copy in stores + outward:
+        copy.wait()
+
+
+def finish(small, fq, fo, fu, fd, act, tgrad):
+    n, D = fo.shape
+    steps = (fq.shape[0] + fo.shape[0] + fu.shape[0] + fd.shape[0]) // n
+    anyspec = pl.BlockSpec(memory_space=pl.ANY)
+    vspec = pl.BlockSpec(memory_space=pltpu.VMEM)
+    sds = jax.ShapeDtypeStruct
+    return pl.pallas_call(
+        finish_kernel,
+        out_shape=[sds((D,), F32)] * 7 + [sds((3, n), F32)]
+        + [sds(v.shape, F32) for v in (fq, fo, fu, fd)]
+        + [sds(v.shape, v.dtype) for v in (act, tgrad)],
+        in_specs=[vspec] + [anyspec] * 6,
+        out_specs=[vspec] * 8 + [anyspec] * 6,
+        scratch_shapes=[
+            pltpu.VMEM((steps, n, D), BF16),
+            pltpu.VMEM((steps, n, D), F32),
+            pltpu.VMEM((2, *act.shape), BF16),
+            pltpu.SemaphoreType.DMA((steps,)),
+            pltpu.SemaphoreType.DMA((steps,)),
+            pltpu.SemaphoreType.DMA((4,)),
+        ],
+        compiler_params=pltpu.CompilerParams(vmem_limit_bytes=61 * 1024 * 1024),
+        name="finish",
+    )(small, fq, fo, fu, fd, act, tgrad)
 
 
 def shards(
@@ -1113,6 +1195,7 @@
             V((T, 2 * T), F32),
             V((T, 2 * T), F32),
             V((T, 2 * T), F32),
+            V((128, 3 * R), BF16),
             V((2 * R, D), BF16),
             V((2 * R, D), BF16),
             V((R, D), BF16),
@@ -1145,20 +1228,17 @@
         down_bias, up_bias, qkv_bias, block_size, tokens, cotangent, wq, wo, wu, wdn,
     )
     act, tgrad, small, fq, fo, fu, fd = outs
-    grads = [
-        jnp.transpose(fq.reshape(3, local_width, D), (2, 0, 1)).astype(F32),
-        fo.reshape(local_width, D).astype(F32),
-        fu.reshape(D, D).astype(F32),
-        fd.reshape(D, D).astype(F32),
-    ]
     if groups > 1:
         ids = [[g * 8 + k for g in range(groups)] for k in range(8)]
-        grads, small = lax.psum((grads, small), "wide", axis_index_groups=ids)
-    gq, go, gu, gd = grads
-    qb, ubias = small[6:9, :local_width], small[9]
-    return (
-        act, tgrad, small[0], small[1], gq, qb, go, small[2], small[3], small[4], gu, ubias, gd, small[5],
+        small = lax.psum(small, "wide", axis_index_groups=ids)
+    g1, s1, ob, g2, s2, db, upb, qkvb, gq, go, gu, gd, act, tgrad = finish(
+        small, fq.reshape(3 * local_width, D), fo.reshape(local_width, D), fu.reshape(D, D),
+        fd.reshape(D, D), act, tgrad,
     )
+    if groups > 1:
+        gq, go, gu, gd = lax.psum((gq, go, gu, gd), "wide", axis_index_groups=ids)
+    gq = jnp.transpose(gq.reshape(3, local_width, D), (2, 0, 1))
+    return act, tgrad, g1, s1, gq, qkvb, go, ob, g2, s2, gu, upb, gd, db
 
 
 def solution(mesh):

time: 196 us -> 193 us (0.985)
  Pallas kernels: 181 us -> 188 us
  other arithmetic: 6.54 us -> 0 us
  local copies, waits for them, and re-layouts: 3.03 us -> 0 us
    convert_element_type x3 -> x0, other arithmetic: 6.54 us -> none  [the longest x1 4.25 us: shards(): fd.reshape(D, D).astype(F32)]
    pallas_call x0 -> x1, Pallas kernels: none -> 6.28 us  [finish(): pl.pallas_call(finish_kernel, out_shape=[sds((D,), F32)] * 7 + [sds((3, n...]
where the time goes in v1:
time: 193 us; the launch traced here: 190 us
  Pallas kernels  188 us (97%)
    pallas_call x1, Pallas kernels, shards(): pl.pallas_call(layer_kernel, out_shape=[sds((R, D), BF16), sds((R, D), BF...  182 us
    pallas_call x1, Pallas kernels, finish(): pl.pallas_call(finish_kernel, out_shape=[sds((D,), F32)] * 7 + [sds((3, n...  6.28 us

profile of v1, /device:TPU:0, one launch (start us, length us, event | category | flops | bytes accessed | tf_op | source)
XLA Modules:
  0.0 189.7 jit_solution(15336108783624389469)
XLA Ops:
  1.3 181.8 %layer.1 = (bf16[512,768]{1,0:T(8,128)(2,1)}, bf16[512,768]{1,0:T(8,128)(2,1)}, f32[16,768]{1,0:T(8,128)}, bf16[3,3,2,2,16,768]{5,4,3,2,1,0:T(8,128)(2,1)}, bf16...) custom-call(f32[1024,128]{1,0:T(8,128)} %constant.4.clone.cos_ref, ...), custom_call_target="tpu_custom_call" | custom-call | tf_op jit(solution)/shard_map/layer/pallas_call | solution.py:1170
  183.1 6.3 %finish.1 = (f32[768]{0:T(1024)}, f32[768]{0:T(1024)}, f32[768]{0:T(1024)}, f32[768]{0:T(1024)}, f32[768]{0:T(1024)}, /*index=5*/f32[768]{0:T(1024)}, f32[768]{0...) custom-call(f32[16,768]{1,0:T(8,128)} %get-tuple-element.35.small_re, ...), custom_call_target="tpu_custom_call" | custom-call | tf_op jit(solution)/shard_map/finish/pallas_call | solution.py:1121

commit v2 on v1

--- a/solution.py
+++ b/solution.py
@@ -219,14 +219,14 @@
         for s in range(2):
             piece = W[g].at[:, s, yy, xx]
             recv(piece, wz_r[g] + s, foreign(s))
-            relayed = 0 if s == 0 else 1
+            relayed = 0 if s == int(g in (O, U1, D1)) else 1
             for j, dev in enumerate((wx, wy)):
                 r = wxy_r[g] + 3 * s + (0 if j == relayed else 2)
                 send(piece, piece, r, (dev, z), foreign(s), w_sent[g])
             send(piece, piece, wz_r[g] + s, (w, far), is_entry, w_sent[g])
 
     def weights_relay(g):
-        along_x = 0
+        along_x = int(g in (O, U1, D1))
         piece = W[g].at[:, along_x, yy, 1 - xx]
         r = wxy_r[g] + 3 * along_x
         recv(piece, r, foreign(along_x))
@@ -239,7 +239,7 @@
 
     def weights_wait(g):
         w_native[g]()
-        along_x = 0
+        along_x = int(g in (O, U1, D1))
         along_y = 1 - along_x
         recv(W[g].at[:, along_x, 1 - yy], wxy_r[g] + 3 * along_x + 2, foreign(along_x))
         recv(W[g].at[:, along_y, :, 1 - xx], wxy_r[g] + 3 * along_y + 2, foreign(along_y))
@@ -1083,7 +1083,7 @@
 def finish_kernel(
     small_ref, q_ref, o_ref, u_ref, d_ref, act_ref, tg_ref,
     g1, s1, ob, g2, s2, db, upb, qkvb, gq, go, gu, gd, act, tg,
-    low, high, kept, ls, ss, cs,
+    low, high, kept, flat, square, ls, ss, cs, vs,
 ):
     n = low.shape[1]
     parts = [
@@ -1097,10 +1097,15 @@
     outward = [pltpu.make_async_copy(kept.at[k], b, cs.at[2 + k]) for k, b in enumerate((act, tg))]
     for load in loads + inward:
         load.start()
-    for k, out in enumerate((g1, s1, ob, g2, s2, db)):
-        out[...] = small_ref[k, :]
-    upb[...] = small_ref[9, :]
-    qkvb[...] = small_ref[6:9, : qkvb.shape[1]]
+    for v, k in zip(flat, (0, 1, 2, 3, 4, 5, 9)):
+        v[...] = small_ref[k, :]
+    square[...] = small_ref[6:9, : qkvb.shape[1]]
+    vectors = [
+        pltpu.make_async_copy(v, out, vs.at[k])
+        for k, (v, out) in enumerate(zip((*flat, square), (g1, s1, ob, g2, s2, db, upb, qkvb)))
+    ]
+    for copy in vectors:
+        copy.start()
     for k, load in enumerate(loads):
         load.wait()
         high[k] = low[k].astype(F32)
@@ -1108,7 +1113,7 @@
     for load, store in zip(inward, outward):
         load.wait()
         store.start()
-    for copy in stores + outward:
+    for copy in stores + outward + vectors:
         copy.wait()
 
 
@@ -1124,14 +1129,17 @@
         + [sds(v.shape, F32) for v in (fq, fo, fu, fd)]
         + [sds(v.shape, v.dtype) for v in (act, tgrad)],
         in_specs=[vspec] + [anyspec] * 6,
-        out_specs=[vspec] * 8 + [anyspec] * 6,
+        out_specs=[anyspec] * 14,
         scratch_shapes=[
             pltpu.VMEM((steps, n, D), BF16),
             pltpu.VMEM((steps, n, D), F32),
             pltpu.VMEM((2, *act.shape), BF16),
+            [pltpu.VMEM((D,), F32)] * 7,
+            pltpu.VMEM((3, n), F32),
             pltpu.SemaphoreType.DMA((steps,)),
             pltpu.SemaphoreType.DMA((steps,)),
             pltpu.SemaphoreType.DMA((4,)),
+            pltpu.SemaphoreType.DMA((8,)),
         ],
         compiler_params=pltpu.CompilerParams(vmem_limit_bytes=61 * 1024 * 1024),
         name="finish",

time: 193 us -> 192 us (level)
  no operation moved by 1% of the time
where the time goes in v2:
time: 192 us; the launch traced here: 189 us
  Pallas kernels  188 us (98%)
    pallas_call x1, Pallas kernels, shards(): pl.pallas_call(layer_kernel, out_shape=[sds((R, D), BF16), sds((R, D), BF...  182 us
    pallas_call x1, Pallas kernels, finish(): pl.pallas_call(finish_kernel, out_shape=[sds((D,), F32)] * 7 + [sds((3, n...  5.75 us

profile of v2, /device:TPU:0, one launch (start us, length us, event | category | flops | bytes accessed | tf_op | source)
XLA Modules:
  0.0 189.3 jit_solution(14047391985195401429)
XLA Ops:
  1.3 181.9 %layer.1 = (bf16[512,768]{1,0:T(8,128)(2,1)}, bf16[512,768]{1,0:T(8,128)(2,1)}, f32[16,768]{1,0:T(8,128)}, bf16[3,3,2,2,16,768]{5,4,3,2,1,0:T(8,128)(2,1)}, bf16...) custom-call(f32[1024,128]{1,0:T(8,128)} %constant.4.clone.cos_ref, ...), custom_call_target="tpu_custom_call" | custom-call | tf_op jit(solution)/shard_map/layer/pallas_call | solution.py:1178
  183.2 5.8 %finish.1 = (f32[768]{0:T(1024)}, f32[768]{0:T(1024)}, f32[768]{0:T(1024)}, f32[768]{0:T(1024)}, f32[768]{0:T(1024)}, /*index=5*/f32[768]{0:T(1024)}, f32[768]{0...) custom-call(f32[16,768]{1,0:T(8,128)} %get-tuple-element.35.small_re, ...), custom_call_target="tpu_custom_call" | custom-call | tf_op jit(solution)/shard_map/finish/pallas_call | solution.py:1126
